TPU v7x, 32 devices: a whole 2x2x4 slice. The times are simulated.
32 devices in a mesh: member: 2 (over x), gx: 16 (over z, y, core).
Axes of the slice: x: 2, y: 2, z: 4, core: 2. Of those that a mesh axis runs over, the one named last changes fastest.
Arguments:
- right_side: float32 [32, 32, 64, 128], P(('member', 'gx')), parts along dimension 0, may hold values from -120 to 120
- cell_kind: int32 [32, 32, 64, 128], P(('member', 'gx')), parts along dimension 0, may hold values from 0 to 4
Outputs:
- solution_field: float32 [32, 32, 64, 128], P(('member', 'gx')), parts along dimension 0
- residual: float32 [32, 32, 64, 128], P(('member', 'gx')), parts along dimension 0
- residual_norms: float32 [4], P('member'), parts along dimension 0
There are 2 independent parts, one for each index of `member`. A program takes and returns all parts, laid end to end along the dimension named above; each array names one. Nothing has to cross between parts.
All inputs are finite; a program needn't handle non-finite values.
Results may differ from a plain program's by a relative error of at most 0.013.
Values sent between devices are 32-bit elements; how exact they have to be, the bound alone decides.
A program may use at most 64 MiB of HBM per device.

v0:
```python
import jax
import jax.numpy as jnp
from jax import lax
from jax.sharding import PartitionSpec as P

GYB = 8
ITERS = 2


CLASS_VALUES = (0.0, 0.5, 1.0, 2.0, 4.0)
SHIFT_TERM = 0.1


def passed_along(value, axis, by):
    peers = lax.axis_size(axis)
    pairs = [(i, i + by) for i in range(peers) if 0 <= i + by < peers]
    return lax.ppermute(value, axis, pairs)


def conductivity_of(cell_kind):
    result = jnp.zeros(cell_kind.shape, jnp.float32)
    for number, value in enumerate(CLASS_VALUES):
        result = result + jnp.where(cell_kind == number, value, 0.0).astype(jnp.float32)
    return result


def harmonic(first, second):
    return 2.0 * first * second / jnp.maximum(first + second, 0.5)


def extend_block(field):
    column = lax.axis_index("gx") % GYB
    low_x = passed_along(field[-1], "gx", GYB)
    high_x = passed_along(field[0], "gx", -GYB)
    low_y = passed_along(field[:, -1], "gx", 1)
    high_y = passed_along(field[:, 0], "gx", -1)
    low_y = jnp.where(column > 0, low_y, 0.0)
    high_y = jnp.where(column < GYB - 1, high_y, 0.0)
    middle = jnp.concatenate([low_x[None], field, high_x[None]], 0)
    low_side = jnp.pad(low_y, ((1, 1), (0, 0)))[:, None]
    high_side = jnp.pad(high_y, ((1, 1), (0, 0)))[:, None]
    grown_field = jnp.concatenate([low_side, middle, high_side], 1)
    return jnp.pad(grown_field, ((0, 0), (0, 0), (1, 1)))


def face_fields(conductivity, padded):
    return (
        harmonic(conductivity, padded[2:, 1:-1, 1:-1]),
        harmonic(conductivity, padded[:-2, 1:-1, 1:-1]),
        harmonic(conductivity, padded[1:-1, 2:, 1:-1]),
        harmonic(conductivity, padded[1:-1, :-2, 1:-1]),
        harmonic(conductivity, padded[1:-1, 1:-1, 2:]),
        harmonic(conductivity, padded[1:-1, 1:-1, :-2]),
    )


def neighbour_sum(face_list, padded):
    total = face_list[0] * padded[2:, 1:-1, 1:-1] + face_list[1] * padded[:-2, 1:-1, 1:-1]
    total = total + face_list[2] * padded[1:-1, 2:, 1:-1] + face_list[3] * padded[1:-1, :-2, 1:-1]
    total = total + face_list[4] * padded[1:-1, 1:-1, 2:] + face_list[5] * padded[1:-1, 1:-1, :-2]
    return total


def operate_field(field, face_list, fluid_mask, diagonal_sum):
    padded = extend_block(field)
    return jnp.where(fluid_mask, diagonal_sum * field - neighbour_sum(face_list, padded), field)


def body(right_side, cell_kind):
    right_block = right_side[0]
    kind_block = cell_kind[0]
    conductivity = conductivity_of(kind_block)
    face_list = face_fields(conductivity, extend_block(conductivity))
    fluid_mask = kind_block > 0
    face_total = (
        face_list[0] + face_list[1] + face_list[2] + face_list[3] + face_list[4] + face_list[5]
    )
    diagonal_sum = jnp.where(fluid_mask, SHIFT_TERM + face_total, 1.0)
    cell_count = (
        lax.axis_size("gx") * right_block.shape[0] * right_block.shape[1] * right_block.shape[2]
    )
    residual = jnp.where(fluid_mask, right_block, 0.0)
    solution_field = jnp.zeros_like(residual)
    smoothed = residual / diagonal_sum
    norms = []
    search = smoothed
    gamma_old = None
    for index_step in range(ITERS):
        gamma_now, res_sq = lax.psum(
            (jnp.sum(residual * smoothed), jnp.sum(residual * residual)), "gx"
        )
        norms.append(res_sq / cell_count)
        if index_step > 0:
            search = smoothed + gamma_now / gamma_old * search
        search_image = operate_field(search, face_list, fluid_mask, diagonal_sum)
        curved = lax.psum(jnp.sum(search * search_image), "gx")
        alpha_now = gamma_now / curved
        solution_field = solution_field + alpha_now * search
        residual = residual - alpha_now * search_image
        smoothed = residual / diagonal_sum
        gamma_old = gamma_now
    return (solution_field[None], residual[None], jnp.stack(norms))


def solution(mesh):
    in_specs = (P(("member", "gx"), None, None, None), P(("member", "gx"), None, None, None))
    out_specs = (
        P(("member", "gx"), None, None, None),
        P(("member", "gx"), None, None, None),
        P("member"),
    )
    return jax.shard_map(body, mesh=mesh, in_specs=in_specs, out_specs=out_specs, check_vma=False)
```

profile of v0, /device:TPU:0, one launch (start us, length us, event | category | flops | bytes accessed | tf_op | source)
XLA Modules:
  0.0 172.2 jit_solution(10122558668228422494)
XLA Ops:
  0.6 1.6 select_add_fusion
  2.9 1.3 collective-permute-start.2
  4.2 3.0 %collective-permute-start.3 = (f32[32,128]{1,0:T(8,128)S(1)}, f32[32,128]{1,0:T(8,128)S(1)}, u32[]{:S(2)}, u32[]{:S(2)}) collective-permute-start(f32[32,128]{1,0:T(8,128)S(1)} %get-tuple-element.32), channel_id=1, source_target_pairs={{0,1},{1,2},{2,3},{3,4},{4,5},{5,6},{6,7},{7,8},{8,9},{9,10},{10,1... | collective-permute-start | bytes 49160 | tf_op jit(solution)/shard_map/ppermute | solution.py:17
  7.2 1.3 collective-permute-start
  8.5 6.3 %collective-permute-start.1 = (f32[64,128]{1,0:T(8,128)S(1)}, f32[64,128]{1,0:T(8,128)S(1)}, u32[]{:S(2)}, u32[]{:S(2)}) collective-permute-start(f32[64,128]{1,0:T(8,128)S(1)} %get-tuple-element.34), channel_id=1, source_target_pairs={{0,8},{1,9},{2,10},{3,11},{4,12},{5,13},{6,14},{7,15},{16,24},{17,... | collective-permute-start | bytes 98312 | tf_op jit(solution)/shard_map/ppermute | solution.py:17
  14.9 1.5 collective-permute-done.1
  17.5 3.3 %add_add_fusion = (f32[32,64,128]{2,0,1:T(8,128)S(1)}, f32[32,64,128]{2,0,1:T(8,128)S(1)}, f32[32,64,128]{2,0,1:T(8,128)S(1)}, f32[32,64,128]{2,0,1:T(8,128)S(1)}) fusion(f32[32,64,128]{2,0,1:T(8,128)S(1)} %bitcast.96, f32[1,64,128]{2,0,1:T(1,128)S(1)} %bitcast.100, f32[1,64,128]{2,0,1:T(1,128)S(1)} %bitcast.104, f32[34,1,128]{2,0,1:T(8,128)S(1)} %pad_bitcast_fusion.4, ...), kind=kLoop, calls=%fused_computation.97 | loop fusion | flops 10485760 | bytes 8488960 | tf_op jit(solution)/shard_map/add | solution.py:78
  22.3 2.5 %collective-permute-start.7 = (f32[32,128]{1,0:T(8,128)S(1)}, f32[32,128]{1,0:T(8,128)S(1)}, u32[]{:S(2)}, u32[]{:S(2)}) collective-permute-start(f32[32,128]{1,0:T(8,128)S(1)} %get-tuple-element.30), channel_id=1, source_target_pairs={{0,1},{1,2},{2,3},{3,4},{4,5},{5,6},{6,7},{7,8},{8,9},{9,10},{10,1... | collective-permute-start | bytes 49160 | tf_op jit(solution)/shard_map/ppermute | solution.py:17
  24.9 1.3 collective-permute-start.6
  26.2 1.3 collective-permute-start.4
  27.5 7.8 %collective-permute-start.5 = (f32[64,128]{1,0:T(8,128)S(1)}, f32[64,128]{1,0:T(8,128)S(1)}, u32[]{:S(2)}, u32[]{:S(2)}) collective-permute-start(f32[64,128]{1,0:T(8,128)S(1)} %get-tuple-element.28), channel_id=1, source_target_pairs={{0,8},{1,9},{2,10},{3,11},{4,12},{5,13},{6,14},{7,15},{16,24},{17,... | collective-permute-start | bytes 98312 | tf_op jit(solution)/shard_map/ppermute | solution.py:17
  37.9 3.6 %fusion.14 = f32[32,64,128]{2,0,1:T(8,128)S(1)} fusion(f32[32,64,128]{2,0,1:T(8,128)S(1)} %get-tuple-element.23, f32[34,66,130]{2,0,1:T(8,128)S(1)} %select_maximum_fusion, f32[32,64,128]{2,0,1:T(8,128)S(1)} %get-tuple-element.22, f32[32,64,128]{2,0,1:T(8,128)S(1)} %get-tuple-element.21, f32[34,1,128]{2,0,1:T(8,128)S(1)} %pad_bitcast_fusion.1, ...), kind=kLoop, calls=%fused_computation.40 | loop fusion | flops 10223616 | bytes 9620480 | tf_op jit(solution)/shard_map/sub | solution.py:66
  42.5 1.7 multiply_reduce_fusion.1
  44.1 33.4 %all-reduce.10 = (f32[]{:T(128)}, f32[]{:T(128)}) all-reduce(f32[]{:T(128)} %get-tuple-element.4, f32[]{:T(128)} %get-tuple-element.5), channel_id=1, replica_groups=mesh['member'=2,'gx'=16] {'gx'}, use_global_device_ids=true, to_apply=%region_1.2 | all-reduce | flops 2 | bytes 16 | tf_op jit(solution)/shard_map/psum | solution.py:89
  78.9 4.2 %multiply_reduce_fusion = (f32[]{:T(128)}, f32[]{:T(128)}, f32[32,64,128]{2,1,0:T(8,128)}, f32[32,64,128]{2,1,0:T(8,128)}) fusion(f32[32,64,128]{2,1,0:T(8,128)S(1)} %get-tuple-element.18, f32[32,64,128]{2,1,0:T(8,128)S(1)} %get-tuple-element.17, f32[32,64,128]{2,0,1:T(8,128)} %copy-done.8, f32[]{:T(128)S(6)} %div.46, f32[1,32,64,128]{3,2,1,0:T(8,128)} %param.2, ...), kind=kLoop, calls=%fused_computation.87 | loop fusion | flops 2359294 | bytes 6553612 | tf_op jit(solution)/shard_map/reduce_sum | solution.py:90
  83.2 30.1 %psum.44 = f32[]{:T(128)} all-reduce(f32[]{:T(128)} %get-tuple-element.7), channel_id=1, replica_groups=mesh['member'=2,'gx'=16] {'gx'}, use_global_device_ids=true, to_apply=%region_5.6 | all-reduce | flops 1 | bytes 8 | tf_op jit(solution)/shard_map/psum | solution.py:89
  114.6 1.4 multiply_add_fusion
  119.2 1.3 collective-permute-start.8
  120.5 3.2 %collective-permute-start.11 = (f32[32,128]{1,0:T(8,128)S(1)}, f32[32,128]{1,0:T(8,128)S(1)}, u32[]{:S(2)}, u32[]{:S(2)}) collective-permute-start(f32[32,128]{1,0:T(8,128)S(1)} %get-tuple-element.26), channel_id=1, source_target_pairs={{0,1},{1,2},{2,3},{3,4},{4,5},{5,6},{6,7},{7,8},{8,9},{9,10},{10,1... | collective-permute-start | bytes 49160 | tf_op jit(solution)/shard_map/ppermute | solution.py:17
  124.5 1.7 collective-permute-done.8
  127.9 1.9 %fusion.9 = f32[32,64,128]{2,0,1:T(8,128)S(1)} fusion(f32[34,1,128]{2,0,1:T(8,128)S(1)} %get-tuple-element.36, f32[34,64,128]{2,0,1:T(8,128)S(1)} %copy.22, f32[32,64,128]{2,0,1:T(8,128)S(1)} %copy.17, f32[1,64,128]{2,0,1:T(1,128)S(1)} %bitcast.109, f32[1,64,128]{2,0,1:T(1,128)S(1)} %bitcast.113, f32[32,64,128]{2,0,1:T(8,128)S(1)} %bitcast.98, ...), kind=kLoop, calls=%fused_computation.32 | loop fusion | flops 6815744 | bytes 4425728 | tf_op jit(solution)/shard_map/add | solution.py:59
  130.1 4.5 %multiply_reduce_fusion.2 = (f32[]{:T(128)}, f32[32,64,128]{2,1,0:T(8,128)}) fusion(f32[32,64,128]{2,1,0:T(8,128)S(1)} %multiply_add_fusion, f32[34,66,130]{2,1,0:T(8,128)S(1)} %select_maximum_fusion.8, f32[32,64,128]{2,0,1:T(8,128)S(1)} %copy-done.7, f32[32,64,128]{2,0,1:T(8,128)S(1)} %copy-done.5, f32[1,64,128]{2,1,0:T(8,128)S(1)} %bitcast.114, ...), kind=kLoop, calls=%fused_computation.91 | loop fusion | flops 3670015 | bytes 9782276 | tf_op jit(solution)/shard_map/reduce_sum | solution.py:96
  134.6 31.4 %all-reduce.9 = (f32[]{:T(128)}, f32[]{:T(128)}, f32[]{:T(128)}) all-reduce(f32[]{:T(128)} %get-tuple-element.13, f32[]{:T(128)} %get-tuple-element.6, f32[]{:T(128)} %get-tuple-element.3), channel_id=1, replica_groups=mesh['member'=2,'gx'=16] {'gx'}, use_global_device_ids=true, to_apply=%region_7.8 | all-reduce | flops 3 | bytes 24 | tf_op jit(solution)/shard_map/psum | solution.py:96
  169.2 3.0 %subtract_bitcast_fusion = (f32[1,32,64,128]{3,2,1,0:T(8,128)}, f32[1,32,64,128]{3,2,1,0:T(8,128)}) fusion(f32[32,64,128]{2,1,0:T(8,128)S(1)} %copy-done.11, f32[32,64,128]{2,1,0:T(8,128)} %get-tuple-element.14, f32[]{:T(128)S(6)} %div.49, f32[32,64,128]{2,1,0:T(8,128)S(1)} %multiply_add_fusion, f32[32,64,128]{2,1,0:T(8,128)S(1)} %get-tuple-element.17, ...), kind=kLoop, calls=%fused_computation.89 | loop fusion | flops 1310720 | bytes 6291464 | tf_op jit(solution)/shard_map/broadcast_in_dim | solution.py:102
  (66 shorter events, 13.2 us)
Async XLA Ops:
  2.9 12.0 %collective-permute-start.2 = (f32[32,128]{1,0:T(8,128)S(1)}, f32[32,128]{1,0:T(8,128)S(1)}, u32[]{:S(2)}, u32[]{:S(2)}) collective-permute-start(f32[32,128]{1,0:T(8,128)S(1)} %get-tuple-element.33), channel_id=1, source_target_pairs={{1,0},{2,1},{3,2},{4,3},{5,4},{6,5},{7,6},{8,7},{9,8},{10,9},{11,1... | collective-permute-start | bytes 49160 | tf_op jit(solution)/shard_map/ppermute | solution.py:17
  4.2 10.7 %collective-permute-start.3 = (f32[32,128]{1,0:T(8,128)S(1)}, f32[32,128]{1,0:T(8,128)S(1)}, u32[]{:S(2)}, u32[]{:S(2)}) collective-permute-start(f32[32,128]{1,0:T(8,128)S(1)} %get-tuple-element.32), channel_id=1, source_target_pairs={{0,1},{1,2},{2,3},{3,4},{4,5},{5,6},{6,7},{7,8},{8,9},{9,10},{10,1... | collective-permute-start | bytes 49160 | tf_op jit(solution)/shard_map/ppermute | solution.py:17
  7.2 7.7 %collective-permute-start = (f32[64,128]{1,0:T(8,128)S(1)}, f32[64,128]{1,0:T(8,128)S(1)}, u32[]{:S(2)}, u32[]{:S(2)}) collective-permute-start(f32[64,128]{1,0:T(8,128)S(1)} %get-tuple-element.35), channel_id=1, source_target_pairs={{8,0},{9,1},{10,2},{11,3},{12,4},{13,5},{14,6},{15,7},{24,16},{25,... | collective-permute-start | bytes 98312 | tf_op jit(solution)/shard_map/ppermute | solution.py:17
  8.5 7.9 %collective-permute-start.1 = (f32[64,128]{1,0:T(8,128)S(1)}, f32[64,128]{1,0:T(8,128)S(1)}, u32[]{:S(2)}, u32[]{:S(2)}) collective-permute-start(f32[64,128]{1,0:T(8,128)S(1)} %get-tuple-element.34), channel_id=1, source_target_pairs={{0,8},{1,9},{2,10},{3,11},{4,12},{5,13},{6,14},{7,15},{16,24},{17,... | collective-permute-start | bytes 98312 | tf_op jit(solution)/shard_map/ppermute | solution.py:17
  17.5 3.4 %copy-start.9 = (f32[1,32,64,128]{3,2,1,0:T(8,128)S(1)}, f32[1,32,64,128]{3,2,1,0:T(8,128)}, u32[]{:S(2)}) copy-start(f32[1,32,64,128]{3,2,1,0:T(8,128)} %param.2) | copy-start | bytes 3145732
  17.5 3.3 %copy-start.10 = (s32[1,32,64,128]{3,2,1,0:T(8,128)S(1)}, s32[1,32,64,128]{3,2,1,0:T(8,128)}, u32[]{:S(2)}) copy-start(s32[1,32,64,128]{3,2,1,0:T(8,128)} %param.3) | copy-start | bytes 3145732
  20.8 17.1 %copy-start.2 = (f32[32,64,128]{2,0,1:T(8,128)}, f32[32,64,128]{2,0,1:T(8,128)S(1)}, u32[]{:S(2)}) copy-start(f32[32,64,128]{2,0,1:T(8,128)S(1)} %get-tuple-element.21) | copy-start | bytes 3145732
  20.8 17.1 %copy-start.4 = (f32[32,64,128]{2,0,1:T(8,128)}, f32[32,64,128]{2,0,1:T(8,128)S(1)}, u32[]{:S(2)}) copy-start(f32[32,64,128]{2,0,1:T(8,128)S(1)} %get-tuple-element.22) | copy-start | bytes 3145732
  20.8 17.1 %copy-start.6 = (f32[32,64,128]{2,0,1:T(8,128)}, f32[32,64,128]{2,0,1:T(8,128)S(1)}, u32[]{:S(2)}) copy-start(f32[32,64,128]{2,0,1:T(8,128)S(1)} %get-tuple-element.23) | copy-start | bytes 3145732
  21.7 57.2 %copy-start = (f32[32,64,128]{2,1,0:T(8,128)}, f32[32,64,128]{2,1,0:T(8,128)S(1)}, u32[]{:S(2)}) copy-start(f32[32,64,128]{2,1,0:T(8,128)S(1)} %get-tuple-element.18) | copy-start | bytes 3145732
  22.3 12.9 %collective-permute-start.7 = (f32[32,128]{1,0:T(8,128)S(1)}, f32[32,128]{1,0:T(8,128)S(1)}, u32[]{:S(2)}, u32[]{:S(2)}) collective-permute-start(f32[32,128]{1,0:T(8,128)S(1)} %get-tuple-element.30), channel_id=1, source_target_pairs={{0,1},{1,2},{2,3},{3,4},{4,5},{5,6},{6,7},{7,8},{8,9},{9,10},{10,1... | collective-permute-start | bytes 49160 | tf_op jit(solution)/shard_map/ppermute | solution.py:17
  24.9 10.4 %collective-permute-start.6 = (f32[32,128]{1,0:T(8,128)S(1)}, f32[32,128]{1,0:T(8,128)S(1)}, u32[]{:S(2)}, u32[]{:S(2)}) collective-permute-start(f32[32,128]{1,0:T(8,128)S(1)} %get-tuple-element.31), channel_id=1, source_target_pairs={{1,0},{2,1},{3,2},{4,3},{5,4},{6,5},{7,6},{8,7},{9,8},{10,9},{11,1... | collective-permute-start | bytes 49160 | tf_op jit(solution)/shard_map/ppermute | solution.py:17
  26.2 9.4 %collective-permute-start.4 = (f32[64,128]{1,0:T(8,128)S(1)}, f32[64,128]{1,0:T(8,128)S(1)}, u32[]{:S(2)}, u32[]{:S(2)}) collective-permute-start(f32[64,128]{1,0:T(8,128)S(1)} %get-tuple-element.29), channel_id=1, source_target_pairs={{8,0},{9,1},{10,2},{11,3},{12,4},{13,5},{14,6},{15,7},{24,16},{25,... | collective-permute-start | bytes 98312 | tf_op jit(solution)/shard_map/ppermute | solution.py:17
  27.5 9.4 %collective-permute-start.5 = (f32[64,128]{1,0:T(8,128)S(1)}, f32[64,128]{1,0:T(8,128)S(1)}, u32[]{:S(2)}, u32[]{:S(2)}) collective-permute-start(f32[64,128]{1,0:T(8,128)S(1)} %get-tuple-element.28), channel_id=1, source_target_pairs={{0,8},{1,9},{2,10},{3,11},{4,12},{5,13},{6,14},{7,15},{16,24},{17,... | collective-permute-start | bytes 98312 | tf_op jit(solution)/shard_map/ppermute | solution.py:17
  41.5 1.0 copy-start.8
  116.6 7.1 %collective-permute-start.10 = (f32[32,128]{1,0:T(8,128)S(1)}, f32[32,128]{1,0:T(8,128)S(1)}, u32[]{:S(2)}, u32[]{:S(2)}) collective-permute-start(f32[32,128]{1,0:T(8,128)S(1)} %get-tuple-element.27), channel_id=1, source_target_pairs={{1,0},{2,1},{3,2},{4,3},{5,4},{6,5},{7,6},{8,7},{9,8},{10,9},{11,1... | collective-permute-start | bytes 49160 | tf_op jit(solution)/shard_map/ppermute | solution.py:17
  117.9 6.5 %collective-permute-start.9 = (f32[64,128]{1,0:T(8,128)S(1)}, f32[64,128]{1,0:T(8,128)S(1)}, u32[]{:S(2)}, u32[]{:S(2)}) collective-permute-start(f32[64,128]{1,0:T(8,128)S(1)} %get-tuple-element.24), channel_id=1, source_target_pairs={{0,8},{1,9},{2,10},{3,11},{4,12},{5,13},{6,14},{7,15},{16,24},{17,... | collective-permute-start | bytes 98312 | tf_op jit(solution)/shard_map/ppermute | solution.py:17
  119.2 6.9 %collective-permute-start.8 = (f32[64,128]{1,0:T(8,128)S(1)}, f32[64,128]{1,0:T(8,128)S(1)}, u32[]{:S(2)}, u32[]{:S(2)}) collective-permute-start(f32[64,128]{1,0:T(8,128)S(1)} %get-tuple-element.25), channel_id=1, source_target_pairs={{8,0},{9,1},{10,2},{11,3},{12,4},{13,5},{14,6},{15,7},{24,16},{25,... | collective-permute-start | bytes 98312 | tf_op jit(solution)/shard_map/ppermute | solution.py:17
  120.5 3.9 %collective-permute-start.11 = (f32[32,128]{1,0:T(8,128)S(1)}, f32[32,128]{1,0:T(8,128)S(1)}, u32[]{:S(2)}, u32[]{:S(2)}) collective-permute-start(f32[32,128]{1,0:T(8,128)S(1)} %get-tuple-element.26), channel_id=1, source_target_pairs={{0,1},{1,2},{2,3},{3,4},{4,5},{5,6},{6,7},{7,8},{8,9},{9,10},{10,1... | collective-permute-start | bytes 49160 | tf_op jit(solution)/shard_map/ppermute | solution.py:17
  127.9 1.9 %copy-start.1 = (f32[32,64,128]{2,1,0:T(8,128)S(1)}, f32[32,64,128]{2,1,0:T(8,128)}, u32[]{:S(2)}) copy-start(f32[32,64,128]{2,1,0:T(8,128)} %copy-done) | copy-start | bytes 3145732
  127.9 1.9 %copy-start.3 = (f32[32,64,128]{2,0,1:T(8,128)S(1)}, f32[32,64,128]{2,0,1:T(8,128)}, u32[]{:S(2)}) copy-start(f32[32,64,128]{2,0,1:T(8,128)} %copy-done.2) | copy-start | bytes 3145732
  127.9 1.9 %copy-start.5 = (f32[32,64,128]{2,0,1:T(8,128)S(1)}, f32[32,64,128]{2,0,1:T(8,128)}, u32[]{:S(2)}) copy-start(f32[32,64,128]{2,0,1:T(8,128)} %copy-done.4) | copy-start | bytes 3145732
  127.9 2.1 %copy-start.7 = (f32[32,64,128]{2,0,1:T(8,128)S(1)}, f32[32,64,128]{2,0,1:T(8,128)}, u32[]{:S(2)}) copy-start(f32[32,64,128]{2,0,1:T(8,128)} %copy-done.6) | copy-start | bytes 3145732
  130.0 39.2 %copy-start.11 = (f32[32,64,128]{2,1,0:T(8,128)S(1)}, f32[32,64,128]{2,1,0:T(8,128)}, u32[]{:S(2)}) copy-start(f32[32,64,128]{2,1,0:T(8,128)} %get-tuple-element.16) | copy-start | bytes 3145732
where the time goes:
time: 173 us; the launch traced here: 172 us
  blocking collectives  95 us (55%)
  starting transfers between devices  31.9 us (18%)
  other arithmetic  29.8 us (17%)
  between operations  6.46 us (4%)
  waiting for transfers between devices  5.27 us (3%)
  local copies, waits for them, and re-layouts  3.82 us (2%)
    psum x2, blocking collectives, body(): lax.psum((jnp.sum(residual * smoothed), jnp.sum(residual * residual)), 'gx')  63.6 us
    ppermute x12, starting transfers between devices, passed_along(): return lax.ppermute(value, axis, pairs)  31.9 us
    psum x1, blocking collectives, body(): curved = lax.psum(jnp.sum(search * search_image), 'gx')  31.4 us
    reduce_sum x2, other arithmetic, body(): jnp.sum(residual * residual)  5.93 us
    ppermute x12, waiting for transfers between devices, passed_along(): return lax.ppermute(value, axis, pairs)  5.27 us
    reduce_sum x1, other arithmetic, body(): curved = lax.psum(jnp.sum(search * search_image), 'gx')  4.51 us
    sub x1, other arithmetic, operate_field(): diagonal_sum * field - neighbour_sum(face_list, padded)  3.56 us
  transfers between devices with their start and end apart: 12, of which 5 were waited for; matrix products, arithmetic and copies ran while one was open for 0% of the time, Pallas kernels for 0%

commit v1 on v0

v1 whole, which is shorter than its diff:
```python
import functools

import jax
import jax.numpy as jnp
from jax import lax
from jax.experimental import pallas as pl
from jax.experimental.pallas import tpu as pltpu
from jax.sharding import PartitionSpec as P

GYB = 8
SHIFT_TERM = 0.1
PAD = 8
MESH = pl.DeviceIdType.MESH


def inverse(value):
    guess = pl.reciprocal(value, approx=True)
    return guess * (2.0 - value * guess)


def conductivity_of(kind):
    power = jnp.left_shift(jnp.ones_like(kind), kind).astype(jnp.float32) * 0.25
    return jnp.where(kind > 0, power, 0.0)


def harmonic(first, second):
    return (2.0 * first) * second * inverse(jnp.maximum(first + second, 0.5))


def fold(value):
    return jnp.sum(value.reshape(-1, 8, value.shape[-1]), axis=0)


def kernel(
    n, kind_hbm, right_hbm, x_ref, r_ref, norm_ref,
    kind, right, cond, face_x, face_y, face_z, inv, smooth, image, scaled, second,
    kind_x, kind_y, send_kind_y, smooth_y, send_smooth_y, scaled_y, send_scaled_y,
    dots, in_sem, send_sem, recv_sem, dot_send, dot_recv,
):
    bx, by, nz = kind.shape
    rows = pl.ds(PAD, by)
    me = lax.axis_index("gx")
    column = lax.rem(me, GYB)
    line = lax.div(me, GYB)
    lines = n // GYB
    receives = (line > 0, line < lines - 1, column > 0, column < GYB - 1)
    sends = (line < lines - 1, line > 0, column < GYB - 1, column > 0)
    targets = (me + GYB, me - GYB, me + 1, me - 1)

    load_kind = pltpu.make_async_copy(kind_hbm.at[0], kind, in_sem.at[0])
    load_right = pltpu.make_async_copy(right_hbm.at[0], right, in_sem.at[1])
    load_kind.start()
    load_right.start()

    barrier = pltpu.get_barrier_semaphore()

    def greet(k, _):
        pl.semaphore_signal(
            barrier, inc=1, device_id={"gx": lax.rem(me + k, n)}, device_id_type=MESH
        )
        return 0

    lax.fori_loop(1, n, greet, 0)

    def copy(phase, side, src, dst):
        return pltpu.make_async_remote_copy(
            src_ref=src, dst_ref=dst,
            send_sem=send_sem.at[phase, side], recv_sem=recv_sem.at[phase, side],
            device_id={"gx": targets[side]}, device_id_type=MESH,
        )

    copies = (
        (
            copy(0, 0, kind_hbm.at[0, bx - 1], kind_x.at[0]),
            copy(0, 1, kind_hbm.at[0, 0], kind_x.at[1]),
            copy(0, 2, send_kind_y.at[1], kind_y.at[0]),
            copy(0, 3, send_kind_y.at[0], kind_y.at[1]),
        ),
        (
            copy(1, 0, smooth.at[bx, rows], smooth.at[0, rows]),
            copy(1, 1, smooth.at[1, rows], smooth.at[bx + 1, rows]),
            copy(1, 2, send_smooth_y.at[1], smooth_y.at[0]),
            copy(1, 3, send_smooth_y.at[0], smooth_y.at[1]),
        ),
        (
            copy(2, 0, scaled.at[bx, rows], scaled.at[0, rows]),
            copy(2, 1, scaled.at[1, rows], scaled.at[bx + 1, rows]),
            copy(2, 2, send_scaled_y.at[1], scaled_y.at[0]),
            copy(2, 3, send_scaled_y.at[0], scaled_y.at[1]),
        ),
    )

    def start(phase, sides):
        for side in sides:
            pl.when(sends[side])(copies[phase][side].start)

    def arrive(phase, sides):
        for side in sides:
            pl.when(receives[side])(copies[phase][side].wait_recv)

    for side in (0, 1):
        @pl.when(jnp.logical_not(receives[side]))
        def _():
            kind_x[side] = jnp.zeros((by, nz), jnp.int32)
            smooth[side * (bx + 1), rows] = jnp.zeros((by, nz), jnp.float32)
            scaled[side * (bx + 1), rows] = jnp.zeros((by, nz), jnp.float32)

        @pl.when(jnp.logical_not(receives[side + 2]))
        def _():
            kind_y[side] = jnp.zeros((bx, 1, nz), jnp.int32)
            smooth_y[side] = jnp.zeros((bx, 1, nz), jnp.float32)
            scaled_y[side] = jnp.zeros((bx, 1, nz), jnp.float32)

    pl.semaphore_wait(barrier, n - 1)
    load_kind.wait()

    def take_edges(i, _):
        send_kind_y[0, i] = kind[i, 0:1, :]
        send_kind_y[1, i] = kind[i, by - 1:by, :]
        return 0

    lax.fori_loop(0, bx, take_edges, 0, unroll=8)
    start(0, (2, 3, 0, 1))

    def conduct(i, _):
        cond[i + 1, rows] = conductivity_of(kind[i])
        return 0

    lax.fori_loop(0, bx, conduct, 0, unroll=2)

    last_lane = lax.broadcasted_iota(jnp.int32, (by, nz), 1) == nz - 1

    def inner_faces(i, _):
        own = cond[i + 1, rows]
        above = jnp.where(last_lane, 0.0, pltpu.roll(own, nz - 1, 1))
        face_z[i] = harmonic(own, above)

        @pl.when(i > 0)
        def _():
            face_x[i] = harmonic(own, cond[i, rows])
        return 0

    lax.fori_loop(0, bx, inner_faces, 0)

    arrive(0, (2, 3))

    def put_kind(i, _):
        cond[i + 1, PAD - 1:PAD, :] = conductivity_of(kind_y[0, i])
        cond[i + 1, PAD + by:PAD + by + 1, :] = conductivity_of(kind_y[1, i])
        return 0

    lax.fori_loop(0, bx, put_kind, 0, unroll=8)
    load_right.wait()
    arrive(0, (0, 1))
    face_x[0] = harmonic(cond[1, rows], conductivity_of(kind_x[0]))
    face_x[bx] = harmonic(cond[bx, rows], conductivity_of(kind_x[1]))

    def prepare(i, sums):
        res_sq, gamma = sums
        own = cond[i + 1, rows]
        face_y[i] = harmonic(
            cond[i + 1, PAD:2 * PAD + by, :], cond[i + 1, PAD - 1:2 * PAD + by - 1, :]
        )
        up = face_z[i]
        total = face_x[i] + face_x[i + 1]
        total = total + (face_y[i, 0:by, :] + face_y[i, 1:by + 1, :])
        total = total + (up + pltpu.roll(up, 1, 1))
        fluid = own > 0.0
        diagonal_inverse = inverse(jnp.where(fluid, SHIFT_TERM + total, 1.0))
        residual = jnp.where(fluid, right[i], 0.0)
        value = residual * diagonal_inverse
        right[i] = residual
        inv[i] = diagonal_inverse
        smooth[i + 1, rows] = value
        send_smooth_y[0, i] = value[0:1, :]
        send_smooth_y[1, i] = value[by - 1:by, :]
        return res_sq + fold(residual * residual), gamma + fold(residual * value)

    def neighbour_sum(field, i):
        own = field[i + 1, rows]
        up = face_z[i]
        total = face_x[i] * field[i, rows] + face_x[i + 1] * field[i + 2, rows]
        total = total + face_y[i, 0:by, :] * field[i + 1, PAD - 1:PAD + by - 1, :]
        total = total + face_y[i, 1:by + 1, :] * field[i + 1, PAD + 1:PAD + by + 1, :]
        total = total + up * pltpu.roll(own, nz - 1, 1) + pltpu.roll(up * own, 1, 1)
        return own, total

    def apply(i, sums):
        delta, cross, square, mu = sums
        own, total = neighbour_sum(smooth, i)
        residual = right[i]
        value = residual - total
        other = value * inv[i]
        image[i] = value
        scaled[i + 1, rows] = other
        send_scaled_y[0, i] = other[0:1, :]
        send_scaled_y[1, i] = other[by - 1:by, :]
        return (
            delta + fold(value * own), cross + fold(residual * value),
            square + fold(value * value), mu + fold(value * other),
        )

    def apply_again(i, nu):
        own, total = neighbour_sum(scaled, i)
        value = image[i] - total
        second[i] = value
        return nu + fold(value * own)

    def spread(buffer, field):
        def put(i, _):
            field[i + 1, PAD - 1:PAD, :] = buffer[0, i]
            field[i + 1, PAD + by:PAD + by + 1, :] = buffer[1, i]
            return 0

        lax.fori_loop(0, bx, put, 0, unroll=8)

    zero = jnp.zeros((8, nz), jnp.float32)
    sums = prepare(bx - 1, prepare(0, (zero, zero)))
    start(1, (0, 1))
    res_sq, gamma = lax.fori_loop(1, bx - 1, prepare, sums)
    start(1, (2, 3))
    arrive(1, (2, 3))
    spread(smooth_y, smooth)
    arrive(1, (0, 1))
    sums = apply(bx - 1, apply(0, (zero,) * 4))
    start(2, (0, 1))
    delta, cross, square, mu = lax.fori_loop(1, bx - 1, apply, sums)
    start(2, (2, 3))
    arrive(2, (2, 3))
    spread(scaled_y, scaled)
    nu = lax.fori_loop(1, bx - 1, apply_again, zero)
    arrive(2, (0, 1))
    nu = apply_again(bx - 1, apply_again(0, nu))

    parts = (res_sq, gamma, delta, cross, square, mu, nu)
    row = lax.broadcasted_iota(jnp.int32, (8, nz), 0)
    message = zero
    for place, part in enumerate(parts):
        message = jnp.where(row == place, jnp.sum(part, axis=0, keepdims=True), message)
    dots[me] = message

    def tell(k, _):
        pltpu.make_async_remote_copy(
            src_ref=dots.at[me], dst_ref=dots.at[me], send_sem=dot_send, recv_sem=dot_recv,
            device_id={"gx": lax.rem(me + k, n)}, device_id_type=MESH,
        ).start()
        return 0

    lax.fori_loop(1, n, tell, 0)
    most = dots.at[pl.ds(0, n - 1)]
    pltpu.make_async_copy(most, most, dot_recv).wait()

    total = jnp.sum(jnp.sum(dots[...], axis=0), axis=1, keepdims=True)
    res_sq, gamma, delta, cross, square, mu, nu = (total[k:k + 1, :] for k in range(7))
    alpha = gamma / delta
    gamma_next = gamma - 2.0 * alpha * delta + alpha * alpha * mu
    delta_next = delta - 2.0 * alpha * mu + alpha * alpha * nu
    res_sq_next = res_sq - 2.0 * alpha * cross + alpha * alpha * square
    beta = gamma_next / gamma
    alpha_next = gamma_next / (delta_next - beta * gamma_next / alpha)
    along = alpha + alpha_next * (1.0 + beta)
    across = alpha * alpha_next
    cells = n * bx * by * nz
    lane = lax.broadcasted_iota(jnp.int32, (1, nz), 1)
    norm_ref[...] = jnp.where(lane == 0, res_sq / cells, res_sq_next / cells)

    along = jnp.broadcast_to(along, (by, nz))
    across = jnp.broadcast_to(across, (by, nz))

    def finish(i, _):
        x_ref[0, i] = along * smooth[i + 1, rows] - across * scaled[i + 1, rows]
        r_ref[0, i] = right[i] - along * image[i] + across * second[i]
        return 0

    lax.fori_loop(0, bx, finish, 0, unroll=2)

    for phase in range(3):
        for side in range(4):
            pl.when(sends[side])(copies[phase][side].wait_send)
    pltpu.make_async_copy(most, most, dot_send).wait()


def body(right_side, cell_kind):
    n = lax.axis_size("gx")
    _, bx, by, nz = right_side.shape
    f32, i32 = jnp.float32, jnp.int32
    field = pltpu.VMEM((bx, by, nz), f32)
    padded = pltpu.VMEM((bx + 2, by + 2 * PAD, nz), f32)
    edges = pltpu.VMEM((2, bx, 1, nz), f32)
    x, r, norms = pl.pallas_call(
        functools.partial(kernel, n),
        out_shape=(
            jax.ShapeDtypeStruct(right_side.shape, f32),
            jax.ShapeDtypeStruct(right_side.shape, f32),
            jax.ShapeDtypeStruct((1, nz), f32),
        ),
        in_specs=[pl.BlockSpec(memory_space=pl.ANY)] * 2,
        out_specs=[pl.BlockSpec(memory_space=pltpu.VMEM)] * 3,
        scratch_shapes=[
            pltpu.VMEM((bx, by, nz), i32), field, padded,
            pltpu.VMEM((bx + 1, by, nz), f32), pltpu.VMEM((bx, by + PAD, nz), f32),
            field, field, padded, field, padded, field,
            pltpu.VMEM((2, by, nz), i32), pltpu.VMEM((2, bx, 1, nz), i32),
            pltpu.VMEM((2, bx, 1, nz), i32), edges, edges, edges, edges,
            pltpu.VMEM((n, 8, nz), f32),
            pltpu.SemaphoreType.DMA((2,)),
            pltpu.SemaphoreType.DMA((3, 4)),
            pltpu.SemaphoreType.DMA((3, 4)),
            pltpu.SemaphoreType.DMA,
            pltpu.SemaphoreType.DMA,
        ],
        compiler_params=pltpu.CompilerParams(
            collective_id=0, has_side_effects=True, vmem_limit_bytes=44 * 1024 * 1024
        ),
    )(cell_kind, right_side)
    return x, r, norms[0, :2]


def solution(mesh):
    spec = P(("member", "gx"), None, None, None)
    return jax.shard_map(
        body, mesh=mesh, in_specs=(spec, spec), out_specs=(spec, spec, P("member")),
        check_vma=False,
    )
```

time: 173 us -> 33.9 us (0.20)
  blocking collectives: 95 us -> 0 us
  starting transfers between devices: 31.9 us -> 0 us
  other arithmetic: 29.8 us -> 0 us
  Pallas kernels: 0 us -> 28.2 us
  between operations: 6.46 us -> 0.65 us
  waiting for transfers between devices: 5.27 us -> 0 us
    psum x3 -> x0, blocking collectives: 95 us -> none  [the longest x2 63.6 us: body(): lax.psum((jnp.sum(residual * smoothed), jnp.sum(residual * residual)), 'gx')]
    ppermute x12 -> x0, starting transfers between devices: 31.9 us -> none  [passed_along(): return lax.ppermute(value, axis, pairs)]
    pallas_call x0 -> x1, Pallas kernels: none -> 28.2 us  [body(): pl.pallas_call(functools.partial(kernel, n), out_shape=(jax.ShapeDtypeStr...]
    reduce_sum x3 -> x0, other arithmetic: 10.4 us -> none  [the longest x2 5.93 us: body(): jnp.sum(residual * residual)]
    add x4 -> x0, other arithmetic: 8.17 us -> none  [the longest x1 3.29 us: body(): diagonal_sum = jnp.where(fluid_mask, SHIFT_TERM + face_total, 1.0)]
    ppermute x12 -> x0, waiting for transfers between devices: 5.27 us -> none  [passed_along(): return lax.ppermute(value, axis, pairs)]
    sub x1 -> x0, other arithmetic: 3.56 us -> none  [operate_field(): diagonal_sum * field - neighbour_sum(face_list, padded)]
    concatenate x4 -> x0, other arithmetic: 3.18 us -> none  [the longest x3 3.06 us: extend_block(): grown_field = jnp.concatenate([low_side, middle, high_side], 1)]
  transfers between devices with their start and end apart: 12 -> 0, of which waited for: 5 -> 0; matrix products, arithmetic and copies ran while one was open for 0% -> 0% of each run, Pallas kernels for 0% -> 0%
where the time goes in v1:
time: 33.9 us; the launch traced here: 33.7 us
  Pallas kernels  28.2 us (83%)
  local copies, waits for them, and re-layouts  4.89 us (14%)
  between operations  0.65 us (2%)
    pallas_call x1, Pallas kernels, body(): pl.pallas_call(functools.partial(kernel, n), out_shape=(jax.ShapeDtypeStr...  28.2 us
    unnamed x6, local copies, waits for them, and re-layouts  4.38 us

profile of v1, /device:TPU:0, one launch (start us, length us, event | category | flops | bytes accessed | tf_op | source)
XLA Modules:
  0.0 33.7 jit_solution(16897010585936928042)
XLA Ops:
  0.6 0.0 copy-start
  0.6 1.2 %copy-done = s32[1,32,64,128]{3,2,1,0:T(8,128)S(1)} copy-done((s32[1,32,64,128]{3,2,1,0:T(8,128)S(1)}, s32[1,32,64,128]{3,2,1,0:T(8,128)}, u32[]{:S(2)}) %copy-start) | copy-done | bytes 1048600
  1.9 0.0 copy-start.1
  1.9 1.2 %copy-done.1 = f32[1,32,64,128]{3,2,1,0:T(8,128)S(1)} copy-done((f32[1,32,64,128]{3,2,1,0:T(8,128)S(1)}, f32[1,32,64,128]{3,2,1,0:T(8,128)}, u32[]{:S(2)}) %copy-start.1) | copy-done | bytes 1048600
  3.1 28.2 %shard_map.49 = (f32[1,32,64,128]{3,2,1,0:T(8,128)S(1)}, f32[1,32,64,128]{3,2,1,0:T(8,128)S(1)}, f32[1,128]{1,0:T(1,128)S(1)}) custom-call(s32[1,32,64,128]{3,2,1,0:T(8,128)S(1)} %copy-done, f32[1,32,64,128]{3,2,1,0:T(8,128)S(1)} %copy-done.1), custom_call_target="tpu_custom_call" | custom-call | tf_op jit(solution)/shard_map/pallas_call | solution.py:290
  31.3 0.5 %slice_bitcast_fusion = f32[2]{0:T(128)} fusion(f32[1,128]{1,0:T(1,128)S(1)} %get-tuple-element.8), kind=kLoop, calls=%fused_computation | loop fusion | bytes 16 | tf_op jit(solution)/shard_map/squeeze | solution.py:316
  31.8 1.0 %copy.7 = f32[1,32,64,128]{3,2,1,0:T(8,128)} copy(f32[1,32,64,128]{3,2,1,0:T(8,128)S(1)} %get-tuple-element.12) | data formatting | bytes 2097152
  32.7 1.0 %copy.8 = f32[1,32,64,128]{3,2,1,0:T(8,128)} copy(f32[1,32,64,128]{3,2,1,0:T(8,128)S(1)} %get-tuple-element.13) | data formatting | bytes 2097152
Async XLA Ops:
  0.6 1.2 %copy-start = (s32[1,32,64,128]{3,2,1,0:T(8,128)S(1)}, s32[1,32,64,128]{3,2,1,0:T(8,128)}, u32[]{:S(2)}) copy-start(s32[1,32,64,128]{3,2,1,0:T(8,128)} %kind_hbm.1) | copy-start | bytes 3145732
  1.9 1.2 %copy-start.1 = (f32[1,32,64,128]{3,2,1,0:T(8,128)S(1)}, f32[1,32,64,128]{3,2,1,0:T(8,128)}, u32[]{:S(2)}) copy-start(f32[1,32,64,128]{3,2,1,0:T(8,128)} %right_hbm.1) | copy-start | bytes 3145732

commit v2 on v1

v2 whole, which is shorter than its diff:
```python
import functools

import jax
import jax.numpy as jnp
from jax import lax
from jax.experimental import pallas as pl
from jax.experimental.pallas import tpu as pltpu
from jax.sharding import PartitionSpec as P

GYB = 8
SHIFT_TERM = 0.1
PAD = 8
INNER_UNROLL = 1
STEP_UNROLL = 2
RIM_UNROLL = 2
MESH = pl.DeviceIdType.MESH


def inverse(value):
    guess = pl.reciprocal(value, approx=True)
    return guess * (2.0 - value * guess)


def conductivity_of(kind):
    power = jnp.left_shift(jnp.ones_like(kind), kind).astype(jnp.float32) * 0.25
    return jnp.where(kind > 0, power, 0.0)


def harmonic(first, second):
    return (2.0 * first) * second * inverse(jnp.maximum(first + second, 0.5))


def fold(value):
    return jnp.sum(value.reshape(-1, 8, value.shape[-1]), axis=0)


def kernel(
    n, kind_hbm, right_hbm, right, smooth, image, scaled, second, factors,
    kind, cond, face_x, face_y, face_z, inv,
    kind_x, smooth_x, scaled_x, kind_y, send_kind_y, smooth_y, send_smooth_y, scaled_y,
    send_scaled_y, dots, in_sem, send_sem, recv_sem, dot_send, dot_recv,
):
    bx, by, nz = kind.shape
    rows = pl.ds(PAD, by)
    me = lax.axis_index("gx")
    column = lax.rem(me, GYB)
    line = lax.div(me, GYB)
    lines = n // GYB
    receives = (line > 0, line < lines - 1, column > 0, column < GYB - 1)
    sends = (line < lines - 1, line > 0, column < GYB - 1, column > 0)
    targets = (me + GYB, me - GYB, me + 1, me - 1)

    barrier = pltpu.get_barrier_semaphore()

    def greet(k, _):
        pl.semaphore_signal(
            barrier, inc=1, device_id={"gx": lax.rem(me + k, n)}, device_id_type=MESH
        )
        return 0

    lax.fori_loop(1, n, greet, 0)

    load_kind = pltpu.make_async_copy(kind_hbm.at[0], kind, in_sem.at[0])
    load_right = pltpu.make_async_copy(right_hbm.at[0], right, in_sem.at[1])
    load_kind.start()
    load_right.start()

    def copy(phase, side, src, dst):
        return pltpu.make_async_remote_copy(
            src_ref=src, dst_ref=dst,
            send_sem=send_sem.at[phase, side], recv_sem=recv_sem.at[phase, side],
            device_id={"gx": targets[side]}, device_id_type=MESH,
        )

    copies = (
        (
            copy(0, 0, kind_hbm.at[0, bx - 1], kind_x.at[0]),
            copy(0, 1, kind_hbm.at[0, 0], kind_x.at[1]),
            copy(0, 2, send_kind_y.at[1], kind_y.at[0]),
            copy(0, 3, send_kind_y.at[0], kind_y.at[1]),
        ),
        (
            copy(1, 0, smooth.at[bx - 1, rows], smooth_x.at[0]),
            copy(1, 1, smooth.at[0, rows], smooth_x.at[1]),
            copy(1, 2, send_smooth_y.at[1], smooth_y.at[0]),
            copy(1, 3, send_smooth_y.at[0], smooth_y.at[1]),
        ),
        (
            copy(2, 0, scaled.at[bx - 1, rows], scaled_x.at[0]),
            copy(2, 1, scaled.at[0, rows], scaled_x.at[1]),
            copy(2, 2, send_scaled_y.at[1], scaled_y.at[0]),
            copy(2, 3, send_scaled_y.at[0], scaled_y.at[1]),
        ),
    )

    def start(phase, sides):
        for side in sides:
            pl.when(sends[side])(copies[phase][side].start)

    def arrive(phase, sides):
        for side in sides:
            pl.when(receives[side])(copies[phase][side].wait_recv)

    for side in (0, 1):
        @pl.when(jnp.logical_not(receives[side]))
        def _():
            kind_x[side] = jnp.zeros((by, nz), jnp.int32)
            smooth_x[side] = jnp.zeros((by, nz), jnp.float32)
            scaled_x[side] = jnp.zeros((by, nz), jnp.float32)

        @pl.when(jnp.logical_not(receives[side + 2]))
        def _():
            kind_y[side] = jnp.zeros((bx, 1, nz), jnp.int32)
            smooth_y[side] = jnp.zeros((bx, 1, nz), jnp.float32)
            scaled_y[side] = jnp.zeros((bx, 1, nz), jnp.float32)

    pl.semaphore_wait(barrier, n - 1)
    start(0, (0, 1))
    load_kind.wait()

    def take_edges(i, _):
        send_kind_y[0, i] = kind[i, 0:1, :]
        send_kind_y[1, i] = kind[i, by - 1:by, :]
        return 0

    lax.fori_loop(0, bx, take_edges, 0, unroll=8)
    start(0, (2, 3))

    def conduct(i, _):
        cond[i, rows] = conductivity_of(kind[i])
        return 0

    lax.fori_loop(0, bx, conduct, 0, unroll=4)

    last_lane = lax.broadcasted_iota(jnp.int32, (by, nz), 1) == nz - 1

    def face_along(i):
        own = cond[i, rows]
        above = jnp.where(last_lane, 0.0, pltpu.roll(own, nz - 1, 1))
        face_z[i] = harmonic(own, above)
        return own

    def inner_faces(i, _):
        own = face_along(i)
        face_x[i] = harmonic(own, cond[i - 1, rows])
        return 0

    face_along(0)
    lax.fori_loop(1, bx, inner_faces, 0, unroll=INNER_UNROLL)

    arrive(0, (2, 3))

    def put_kind(i, _):
        cond[i, PAD - 1:PAD, :] = conductivity_of(kind_y[0, i])
        cond[i, PAD + by:PAD + by + 1, :] = conductivity_of(kind_y[1, i])
        return 0

    lax.fori_loop(0, bx, put_kind, 0, unroll=8)
    load_right.wait()

    def prepare(i, sums):
        res_sq, gamma = sums
        own = cond[i, rows]
        face_y[i] = harmonic(
            cond[i, PAD:2 * PAD + by, :], cond[i, PAD - 1:2 * PAD + by - 1, :]
        )
        up = face_z[i]
        total = face_x[i] + face_x[i + 1]
        total = total + (face_y[i, 0:by, :] + face_y[i, 1:by + 1, :])
        total = total + (up + pltpu.roll(up, 1, 1))
        fluid = own > 0.0
        diagonal_inverse = inverse(jnp.where(fluid, SHIFT_TERM + total, 1.0))
        residual = jnp.where(fluid, right[i], 0.0)
        value = residual * diagonal_inverse
        right[i] = residual
        inv[i] = diagonal_inverse
        smooth[i, rows] = value
        send_smooth_y[0, i] = value[0:1, :]
        send_smooth_y[1, i] = value[by - 1:by, :]
        return res_sq + fold(residual * residual), gamma + fold(residual * value)

    def neighbour_sum(field, i, first, count, below, above):
        own = field[i, pl.ds(PAD + first, count)]
        here = pl.ds(first, count)
        up = face_z[i, here]
        total = face_x[i, here] * below + face_x[i + 1, here] * above
        total = total + face_y[i, here] * field[i, pl.ds(PAD + first - 1, count)]
        total = total + face_y[i, pl.ds(first + 1, count)] * field[i, pl.ds(PAD + first + 1, count)]
        total = total + up * pltpu.roll(own, nz - 1, 1) + pltpu.roll(up * own, 1, 1)
        return own, total

    def apply(i, sums, first=0, count=by, below=None, above=None):
        delta, cross, square, mu = sums
        here, inside = pl.ds(first, count), pl.ds(PAD + first, count)
        below = smooth[i - 1, inside] if below is None else below
        above = smooth[i + 1, inside] if above is None else above
        own, total = neighbour_sum(smooth, i, first, count, below, above)
        residual = right[i, here]
        value = residual - total
        other = value * inv[i, here]
        image[i, here] = value
        scaled[i, inside] = other
        if first == 0:
            send_scaled_y[0, i] = other[0:1, :]
        if first + count == by:
            send_scaled_y[1, i] = other[count - 1:count, :]
        return (
            delta + fold(value * own), cross + fold(residual * value),
            square + fold(value * value), mu + fold(value * other),
        )

    def apply_again(i, nu, first=0, count=by, below=None, above=None):
        here, inside = pl.ds(first, count), pl.ds(PAD + first, count)
        below = scaled[i - 1, inside] if below is None else below
        above = scaled[i + 1, inside] if above is None else above
        own, total = neighbour_sum(scaled, i, first, count, below, above)
        value = image[i, here] - total
        second[i, here] = value
        return nu + fold(value * own)

    def spread(buffer, field):
        def put(i, _):
            field[i, PAD - 1:PAD, :] = buffer[0, i]
            field[i, PAD + by:PAD + by + 1, :] = buffer[1, i]
            return 0

        lax.fori_loop(0, bx, put, 0, unroll=8)

    def middle(step, sums):
        return lax.fori_loop(
            1, bx - 1, lambda i, s: step(i, s, PAD, by - 2 * PAD), sums, unroll=STEP_UNROLL
        )

    def rims(step, sums):
        def both(i, s):
            return step(i, step(i, s, 0, PAD), by - PAD, PAD)

        return lax.fori_loop(1, bx - 1, both, sums, unroll=RIM_UNROLL)

    def ends(step, sums, field, halo):
        sums = step(0, sums, below=halo[0])
        return step(bx - 1, sums, above=halo[1])

    zero = jnp.zeros((8, nz), jnp.float32)
    sums = lax.fori_loop(1, bx - 1, prepare, (zero, zero), unroll=STEP_UNROLL)
    arrive(0, (0, 1))
    face_x[0] = harmonic(cond[0, rows], conductivity_of(kind_x[0]))
    face_x[bx] = harmonic(cond[bx - 1, rows], conductivity_of(kind_x[1]))
    res_sq, gamma = prepare(bx - 1, prepare(0, sums))
    start(1, (0, 1, 2, 3))
    sums = middle(apply, (zero,) * 4)
    arrive(1, (2, 3))
    spread(smooth_y, smooth)
    sums = rims(apply, sums)
    arrive(1, (0, 1))
    delta, cross, square, mu = ends(apply, sums, smooth, smooth_x)
    start(2, (0, 1, 2, 3))
    nu = middle(apply_again, zero)
    arrive(2, (2, 3))
    spread(scaled_y, scaled)
    nu = rims(apply_again, nu)
    arrive(2, (0, 1))
    nu = ends(apply_again, nu, scaled, scaled_x)

    parts = (res_sq, gamma, delta, cross, square, mu, nu)
    row = lax.broadcasted_iota(jnp.int32, (8, nz), 0)
    message = zero
    for place, part in enumerate(parts):
        message = jnp.where(row == place, jnp.sum(part, axis=0, keepdims=True), message)
    dots[me] = message

    def tell(k, _):
        pltpu.make_async_remote_copy(
            src_ref=dots.at[me], dst_ref=dots.at[me], send_sem=dot_send, recv_sem=dot_recv,
            device_id={"gx": lax.rem(me + k, n)}, device_id_type=MESH,
        ).start()
        return 0

    lax.fori_loop(1, n, tell, 0)
    most = dots.at[pl.ds(0, n - 1)]
    for phase in range(3):
        for side in range(4):
            pl.when(sends[side])(copies[phase][side].wait_send)
    pltpu.make_async_copy(most, most, dot_recv).wait()

    total = jnp.sum(jnp.sum(dots[...], axis=0), axis=1, keepdims=True)
    res_sq, gamma, delta, cross, square, mu, nu = (total[k:k + 1, :] for k in range(7))
    alpha = gamma / delta
    gamma_next = gamma - 2.0 * alpha * delta + alpha * alpha * mu
    delta_next = delta - 2.0 * alpha * mu + alpha * alpha * nu
    res_sq_next = res_sq - 2.0 * alpha * cross + alpha * alpha * square
    beta = gamma_next / gamma
    alpha_next = gamma_next / (delta_next - beta * gamma_next / alpha)
    along = alpha + alpha_next * (1.0 + beta)
    across = alpha * alpha_next
    cells = n * bx * by * nz
    result = jnp.where(row == 0, along, across)
    result = jnp.where(row == 2, res_sq / cells, result)
    factors[...] = jnp.where(row == 3, res_sq_next / cells, result)
    pltpu.make_async_copy(most, most, dot_send).wait()


def finish(right, smooth, image, scaled, second, factors, x_hbm, r_hbm, norms, x, r, sems):
    bx, by, nz = right.shape
    pieces = sems.shape[1]
    depth = bx // pieces
    along = jnp.broadcast_to(factors[0:1, :], (by, nz))
    across = jnp.broadcast_to(factors[1:2, :], (by, nz))
    rows = pl.ds(PAD, by)
    copies = []
    for piece in range(pieces):
        def combine(i, _):
            x[i] = along * smooth[i, rows] - across * scaled[i, rows]
            r[i] = right[i] - along * image[i] + across * second[i]
            return 0

        lax.fori_loop(piece * depth, (piece + 1) * depth, combine, 0, unroll=2)
        part = pl.ds(piece * depth, depth)
        copies.append(pltpu.make_async_copy(x.at[part], x_hbm.at[0, part], sems.at[0, piece]))
        copies.append(pltpu.make_async_copy(r.at[part], r_hbm.at[0, part], sems.at[1, piece]))
        copies[-2].start()
        copies[-1].start()
    norms[0] = jnp.max(factors[2:3, :])
    norms[1] = jnp.max(factors[3:4, :])
    for copy in copies:
        copy.wait()


def body(right_side, cell_kind):
    n = lax.axis_size("gx")
    _, bx, by, nz = right_side.shape
    f32, i32 = jnp.float32, jnp.int32
    shape = (bx, by, nz)
    padded = (bx, by + 2 * PAD, nz)
    field = pltpu.VMEM(shape, f32)
    planes = pltpu.VMEM((2, by, nz), f32)
    edges = pltpu.VMEM((2, bx, 1, nz), f32)
    fields = pl.pallas_call(
        functools.partial(kernel, n),
        out_shape=tuple(
            jax.ShapeDtypeStruct(s, f32) for s in (shape, padded, shape, padded, shape, (8, nz))
        ),
        in_specs=[pl.BlockSpec(memory_space=pltpu.HBM)] * 2,
        out_specs=[pl.BlockSpec(memory_space=pltpu.VMEM)] * 6,
        scratch_shapes=[
            pltpu.VMEM(shape, i32), pltpu.VMEM(padded, f32),
            pltpu.VMEM((bx + 1, by, nz), f32), pltpu.VMEM((bx, by + PAD, nz), f32),
            field, field,
            pltpu.VMEM((2, by, nz), i32), planes, planes,
            pltpu.VMEM((2, bx, 1, nz), i32), pltpu.VMEM((2, bx, 1, nz), i32),
            edges, edges, edges, edges,
            pltpu.VMEM((n, 8, nz), f32),
            pltpu.SemaphoreType.DMA((2,)),
            pltpu.SemaphoreType.DMA((3, 4)),
            pltpu.SemaphoreType.DMA((3, 4)),
            pltpu.SemaphoreType.DMA,
            pltpu.SemaphoreType.DMA,
        ],
        compiler_params=pltpu.CompilerParams(
            collective_id=0, has_side_effects=True, vmem_limit_bytes=32 * 1024 * 1024
        ),
    )(cell_kind, right_side)
    x, r, norms = pl.pallas_call(
        finish,
        out_shape=(
            jax.ShapeDtypeStruct(right_side.shape, f32),
            jax.ShapeDtypeStruct(right_side.shape, f32),
            jax.ShapeDtypeStruct((2,), f32),
        ),
        in_specs=[pl.BlockSpec(memory_space=pltpu.VMEM)] * 6,
        out_specs=(
            pl.BlockSpec(memory_space=pltpu.HBM), pl.BlockSpec(memory_space=pltpu.HBM),
            pl.BlockSpec(memory_space=pltpu.SMEM),
        ),
        scratch_shapes=[field, field, pltpu.SemaphoreType.DMA((2, 4))],
        compiler_params=pltpu.CompilerParams(vmem_limit_bytes=16 * 1024 * 1024),
    )(*fields)
    return x, r, norms


def solution(mesh):
    spec = P(("member", "gx"), None, None, None)
    return jax.shard_map(
        body, mesh=mesh, in_specs=(spec, spec), out_specs=(spec, spec, P("member")),
        check_vma=False,
    )
```

time: 33.9 us -> 28 us (0.83)
  Pallas kernels: 28.2 us -> 24.8 us
  local copies, waits for them, and re-layouts: 4.89 us -> 2.44 us
    pallas_call x1 -> x2, Pallas kernels: 28.2 us -> 24.8 us  [the longest x1 22.8 us: body(): pl.pallas_call(functools.partial(kernel, n), out_shape=tuple((jax.ShapeDt...]
    unnamed x6 -> x4, local copies, waits for them, and re-layouts: 4.38 us -> 2.44 us
    squeeze x1 -> x0, local copies, waits for them, and re-layouts: 0.51 us -> none  [body(): return (x, r, norms[0, :2])]
where the time goes in v2:
time: 28 us; the launch traced here: 27.8 us
  Pallas kernels  24.8 us (89%)
  local copies, waits for them, and re-layouts  2.44 us (9%)
  between operations  0.65 us (2%)
    pallas_call x1, Pallas kernels, body(): pl.pallas_call(functools.partial(kernel, n), out_shape=tuple((jax.ShapeDt...  22.8 us
    unnamed x4, local copies, waits for them, and re-layouts  2.44 us
    pallas_call x1, Pallas kernels, body(): pl.pallas_call(finish, out_shape=(jax.ShapeDtypeStruct(right_side.shape,...  1.97 us

profile of v2, /device:TPU:0, one launch (start us, length us, event | category | flops | bytes accessed | tf_op | source)
XLA Modules:
  0.0 27.8 jit_solution(16553537456176201096)
XLA Ops:
  0.6 0.0 copy-start
  0.6 1.2 %copy-done = s32[1,32,64,128]{3,2,1,0:T(8,128)S(1)} copy-done((s32[1,32,64,128]{3,2,1,0:T(8,128)S(1)}, s32[1,32,64,128]{3,2,1,0:T(8,128)}, u32[]{:S(2)}) %copy-start) | copy-done | bytes 1048600
  1.9 0.0 copy-start.1
  1.9 1.2 %copy-done.1 = f32[1,32,64,128]{3,2,1,0:T(8,128)S(1)} copy-done((f32[1,32,64,128]{3,2,1,0:T(8,128)S(1)}, f32[1,32,64,128]{3,2,1,0:T(8,128)}, u32[]{:S(2)}) %copy-start.1) | copy-done | bytes 1048600
  3.1 22.8 %shard_map.49 = (f32[32,64,128]{2,1,0:T(8,128)S(1)}, f32[32,80,128]{2,1,0:T(8,128)S(1)}, f32[32,64,128]{2,1,0:T(8,128)S(1)}, f32[32,80,128]{2,1,0:T(8,128)S(1)},...) custom-call(s32[1,32,64,128]{3,2,1,0:T(8,128)S(1)} %copy-done, f32[1,32,64,128]{3,2,1,0:T(8,128)S(1)} %copy-done.1), custom_call_target="tpu_custom_call" | custom-call | tf_op jit(solution)/shard_map/pallas_call | solution.py:338
  25.9 2.0 %shard_map.50 = (f32[1,32,64,128]{3,2,1,0:T(8,128)}, f32[1,32,64,128]{3,2,1,0:T(8,128)}, f32[2]{0:T(128)}) custom-call(f32[32,64,128]{2,1,0:T(8,128)S(1)} %get-tuple-element.9.right, f32[32,80,128]{2,1,0:T(8,128)S(1)} %get-tuple-element.10.smooth, f32[32,64,128]{2,1,0:T(8,128)S(1)} %get-tuple-element.11.image, f32[32,80,128]{2,1,0:T(8,128)S(1)} %get-tuple-element.12.scaled, ...), custom_call_target="tpu_custom_call" | custom-call | tf_op jit(solution)/shard_map/pallas_call | solution.py:363
Async XLA Ops:
  0.6 1.2 %copy-start = (s32[1,32,64,128]{3,2,1,0:T(8,128)S(1)}, s32[1,32,64,128]{3,2,1,0:T(8,128)}, u32[]{:S(2)}) copy-start(s32[1,32,64,128]{3,2,1,0:T(8,128)} %kind_hbm.1) | copy-start | bytes 3145732
  1.9 1.2 %copy-start.1 = (f32[1,32,64,128]{3,2,1,0:T(8,128)S(1)}, f32[1,32,64,128]{3,2,1,0:T(8,128)}, u32[]{:S(2)}) copy-start(f32[1,32,64,128]{3,2,1,0:T(8,128)} %right_hbm.1) | copy-start | bytes 3145732

commit v3 on v2

--- a/solution.py
+++ b/solution.py
@@ -10,9 +10,9 @@
 GYB = 8
 SHIFT_TERM = 0.1
 PAD = 8
-INNER_UNROLL = 1
-STEP_UNROLL = 2
-RIM_UNROLL = 2
+INNER_UNROLL = 4
+STEP_UNROLL = 5
+RIM_UNROLL = 5
 MESH = pl.DeviceIdType.MESH
 
 
@@ -37,8 +37,9 @@
 def kernel(
     n, kind_hbm, right_hbm, right, smooth, image, scaled, second, factors,
     kind, cond, face_x, face_y, face_z, inv,
-    kind_x, smooth_x, scaled_x, kind_y, send_kind_y, smooth_y, send_smooth_y, scaled_y,
-    send_scaled_y, dots, in_sem, send_sem, recv_sem, dot_send, dot_recv,
+    kind_x, right_x, smooth_x, scaled_x, kind_y, send_kind_y, right_y, send_right_y, cond_y,
+    smooth_y, scaled_y, send_scaled_y, corner, send_corner, rim_x, rim_y,
+    dots, in_sem, send_sem, recv_sem, dot_send, dot_recv,
 ):
     bx, by, nz = kind.shape
     rows = pl.ds(PAD, by)
@@ -46,9 +47,14 @@
     column = lax.rem(me, GYB)
     line = lax.div(me, GYB)
     lines = n // GYB
-    receives = (line > 0, line < lines - 1, column > 0, column < GYB - 1)
-    sends = (line < lines - 1, line > 0, column < GYB - 1, column > 0)
-    targets = (me + GYB, me - GYB, me + 1, me - 1)
+    receives = [line > 0, line < lines - 1, column > 0, column < GYB - 1]
+    sends = [line < lines - 1, line > 0, column < GYB - 1, column > 0]
+    targets = [me + GYB, me - GYB, me + 1, me - 1]
+    for low in (0, 1):
+        for left in (2, 3):
+            receives.append(jnp.logical_and(receives[low], receives[left]))
+            sends.append(jnp.logical_and(sends[low], sends[left]))
+            targets.append(targets[low] + targets[left] - me)
 
     barrier = pltpu.get_barrier_semaphore()
 
@@ -65,66 +71,88 @@
     load_kind.start()
     load_right.start()
 
-    def copy(phase, side, src, dst):
-        return pltpu.make_async_remote_copy(
-            src_ref=src, dst_ref=dst,
-            send_sem=send_sem.at[phase, side], recv_sem=recv_sem.at[phase, side],
+    copies = []
+
+    def copy(side, src, dst):
+        place = len(copies)
+        copies.append((side, pltpu.make_async_remote_copy(
+            src_ref=src, dst_ref=dst, send_sem=send_sem.at[place], recv_sem=recv_sem.at[place],
             device_id={"gx": targets[side]}, device_id_type=MESH,
-        )
-
-    copies = (
-        (
-            copy(0, 0, kind_hbm.at[0, bx - 1], kind_x.at[0]),
-            copy(0, 1, kind_hbm.at[0, 0], kind_x.at[1]),
-            copy(0, 2, send_kind_y.at[1], kind_y.at[0]),
-            copy(0, 3, send_kind_y.at[0], kind_y.at[1]),
-        ),
-        (
-            copy(1, 0, smooth.at[bx - 1, rows], smooth_x.at[0]),
-            copy(1, 1, smooth.at[0, rows], smooth_x.at[1]),
-            copy(1, 2, send_smooth_y.at[1], smooth_y.at[0]),
-            copy(1, 3, send_smooth_y.at[0], smooth_y.at[1]),
-        ),
-        (
-            copy(2, 0, scaled.at[bx - 1, rows], scaled_x.at[0]),
-            copy(2, 1, scaled.at[0, rows], scaled_x.at[1]),
-            copy(2, 2, send_scaled_y.at[1], scaled_y.at[0]),
-            copy(2, 3, send_scaled_y.at[0], scaled_y.at[1]),
-        ),
-    )
-
-    def start(phase, sides):
-        for side in sides:
-            pl.when(sends[side])(copies[phase][side].start)
-
-    def arrive(phase, sides):
-        for side in sides:
-            pl.when(receives[side])(copies[phase][side].wait_recv)
+        )))
+
+    copy(0, kind_hbm.at[0, pl.ds(bx - 2, 2)], kind_x.at[0])
+    copy(1, kind_hbm.at[0, pl.ds(0, 2)], kind_x.at[1])
+    copy(2, send_kind_y.at[1], kind_y.at[0])
+    copy(3, send_kind_y.at[0], kind_y.at[1])
+    copy(0, right_hbm.at[0, bx - 1], right_x.at[0])
+    copy(1, right_hbm.at[0, 0], right_x.at[1])
+    copy(2, send_right_y.at[1], right_y.at[0])
+    copy(3, send_right_y.at[0], right_y.at[1])
+    for along_x in (0, 1):
+        for along_y in (0, 1):
+            copy(
+                4 + 2 * along_x + along_y,
+                send_corner.at[1 - along_x, 1 - along_y], corner.at[along_x, along_y],
+            )
+    copy(0, scaled.at[bx - 1, rows], scaled_x.at[0])
+    copy(1, scaled.at[0, rows], scaled_x.at[1])
+    copy(2, send_scaled_y.at[1], scaled_y.at[0])
+    copy(3, send_scaled_y.at[0], scaled_y.at[1])
+
+    def start(places):
+        for place in places:
+            side, item = copies[place]
+            pl.when(sends[side])(item.start)
+
+    def arrive(places):
+        for place in places:
+            side, item = copies[place]
+            pl.when(receives[side])(item.wait_recv)
 
     for side in (0, 1):
         @pl.when(jnp.logical_not(receives[side]))
         def _():
-            kind_x[side] = jnp.zeros((by, nz), jnp.int32)
-            smooth_x[side] = jnp.zeros((by, nz), jnp.float32)
+            kind_x[side] = jnp.zeros((2, by, nz), jnp.int32)
+            right_x[side] = jnp.zeros((by, nz), jnp.float32)
             scaled_x[side] = jnp.zeros((by, nz), jnp.float32)
 
         @pl.when(jnp.logical_not(receives[side + 2]))
         def _():
-            kind_y[side] = jnp.zeros((bx, 1, nz), jnp.int32)
-            smooth_y[side] = jnp.zeros((bx, 1, nz), jnp.float32)
-            scaled_y[side] = jnp.zeros((bx, 1, nz), jnp.float32)
+            kind_y[side] = jnp.zeros((2, bx, nz), jnp.int32)
+            right_y[side] = jnp.zeros((bx, nz), jnp.float32)
+            scaled_y[side] = jnp.zeros((bx, nz), jnp.float32)
+
+        for other in (0, 1):
+            @pl.when(jnp.logical_not(receives[4 + 2 * side + other]))
+            def _():
+                corner[side, other] = jnp.zeros((1, nz), jnp.int32)
 
     pl.semaphore_wait(barrier, n - 1)
-    start(0, (0, 1))
+    start((0, 1, 4, 5))
     load_kind.wait()
 
-    def take_edges(i, _):
-        send_kind_y[0, i] = kind[i, 0:1, :]
-        send_kind_y[1, i] = kind[i, by - 1:by, :]
-        return 0
-
-    lax.fori_loop(0, bx, take_edges, 0, unroll=8)
-    start(0, (2, 3))
+    def take_kind(i, _):
+        one = pl.ds(i, 1)
+        send_kind_y[0, 0, one, :] = kind[i, 0:1, :]
+        send_kind_y[0, 1, one, :] = kind[i, 1:2, :]
+        send_kind_y[1, 0, one, :] = kind[i, by - 1:by, :]
+        send_kind_y[1, 1, one, :] = kind[i, by - 2:by - 1, :]
+        return 0
+
+    lax.fori_loop(0, bx, take_kind, 0, unroll=8)
+    for side in (0, 1):
+        for other in (0, 1):
+            send_corner[side, other] = send_kind_y[other, 0, side * (bx - 1):side * (bx - 1) + 1, :]
+    start((2, 3, 8, 9, 10, 11))
+    load_right.wait()
+
+    def take_right(i, _):
+        send_right_y[0, pl.ds(i, 1), :] = right[i, 0:1, :]
+        send_right_y[1, pl.ds(i, 1), :] = right[i, by - 1:by, :]
+        return 0
+
+    lax.fori_loop(0, bx, take_right, 0, unroll=8)
+    start((6, 7))
 
     def conduct(i, _):
         cond[i, rows] = conductivity_of(kind[i])
@@ -132,12 +160,13 @@
 
     lax.fori_loop(0, bx, conduct, 0, unroll=4)
 
-    last_lane = lax.broadcasted_iota(jnp.int32, (by, nz), 1) == nz - 1
+    def faces_up(own):
+        last_lane = lax.broadcasted_iota(jnp.int32, own.shape, 1) == nz - 1
+        return harmonic(own, jnp.where(last_lane, 0.0, pltpu.roll(own, nz - 1, 1)))
 
     def face_along(i):
         own = cond[i, rows]
-        above = jnp.where(last_lane, 0.0, pltpu.roll(own, nz - 1, 1))
-        face_z[i] = harmonic(own, above)
+        face_z[i] = faces_up(own)
         return own
 
     def inner_faces(i, _):
@@ -148,15 +177,18 @@
     face_along(0)
     lax.fori_loop(1, bx, inner_faces, 0, unroll=INNER_UNROLL)
 
-    arrive(0, (2, 3))
-
-    def put_kind(i, _):
-        cond[i, PAD - 1:PAD, :] = conductivity_of(kind_y[0, i])
-        cond[i, PAD + by:PAD + by + 1, :] = conductivity_of(kind_y[1, i])
-        return 0
-
-    lax.fori_loop(0, bx, put_kind, 0, unroll=8)
-    load_right.wait()
+    def spread(buffer, field):
+        def put(i, _):
+            field[i, PAD - 1:PAD, :] = buffer[0, pl.ds(i, 1), :]
+            field[i, PAD + by:PAD + by + 1, :] = buffer[1, pl.ds(i, 1), :]
+            return 0
+
+        lax.fori_loop(0, bx, put, 0, unroll=8)
+
+    arrive((2, 3))
+    for side in (0, 1):
+        cond_y[side] = conductivity_of(kind_y[side, 0])
+    spread(cond_y, cond)
 
     def prepare(i, sums):
         res_sq, gamma = sums
@@ -175,8 +207,6 @@
         right[i] = residual
         inv[i] = diagonal_inverse
         smooth[i, rows] = value
-        send_smooth_y[0, i] = value[0:1, :]
-        send_smooth_y[1, i] = value[by - 1:by, :]
         return res_sq + fold(residual * residual), gamma + fold(residual * value)
 
     def neighbour_sum(field, i, first, count, below, above):
@@ -201,9 +231,9 @@
         image[i, here] = value
         scaled[i, inside] = other
         if first == 0:
-            send_scaled_y[0, i] = other[0:1, :]
+            send_scaled_y[0, pl.ds(i, 1), :] = other[0:1, :]
         if first + count == by:
-            send_scaled_y[1, i] = other[count - 1:count, :]
+            send_scaled_y[1, pl.ds(i, 1), :] = other[count - 1:count, :]
         return (
             delta + fold(value * own), cross + fold(residual * value),
             square + fold(value * value), mu + fold(value * other),
@@ -218,13 +248,19 @@
         second[i, here] = value
         return nu + fold(value * own)
 
-    def spread(buffer, field):
-        def put(i, _):
-            field[i, PAD - 1:PAD, :] = buffer[0, i]
-            field[i, PAD + by:PAD + by + 1, :] = buffer[1, i]
-            return 0
-
-        lax.fori_loop(0, bx, put, 0, unroll=8)
+    def halo(near, far, own, corners, source, rim):
+        length = near.shape[0]
+        rim[PAD:PAD + length, :] = near
+        rim[PAD - 1:PAD, :] = conductivity_of(corners[0])
+        rim[PAD + length:PAD + length + 1, :] = conductivity_of(corners[1])
+        inner = harmonic(own, near)
+        up = faces_up(near)
+        total = inner + harmonic(near, far) + (up + pltpu.roll(up, 1, 1))
+        total = total + harmonic(near, rim[PAD - 1:PAD - 1 + length, :])
+        total = total + harmonic(near, rim[PAD + 1:PAD + 1 + length, :])
+        fluid = near > 0.0
+        value = jnp.where(fluid, source, 0.0) * inverse(jnp.where(fluid, SHIFT_TERM + total, 1.0))
+        return inner, value
 
     def middle(step, sums):
         return lax.fori_loop(
@@ -243,23 +279,29 @@
 
     zero = jnp.zeros((8, nz), jnp.float32)
     sums = lax.fori_loop(1, bx - 1, prepare, (zero, zero), unroll=STEP_UNROLL)
-    arrive(0, (0, 1))
-    face_x[0] = harmonic(cond[0, rows], conductivity_of(kind_x[0]))
-    face_x[bx] = harmonic(cond[bx - 1, rows], conductivity_of(kind_x[1]))
+    arrive((8, 9, 10, 11, 6, 7))
+    for side in (0, 1):
+        _, smooth_y[side] = halo(
+            cond_y[side], conductivity_of(kind_y[side, 1]), conductivity_of(send_kind_y[side, 0]),
+            (corner[0, side], corner[1, side]), right_y[side], rim_y,
+        )
+    spread(smooth_y, smooth)
+    arrive((0, 1, 4, 5))
+    for side in (0, 1):
+        face_x[side * bx], smooth_x[side] = halo(
+            conductivity_of(kind_x[side, 1 - side]), conductivity_of(kind_x[side, side]),
+            cond[side * (bx - 1), rows], (corner[side, 0], corner[side, 1]), right_x[side], rim_x,
+        )
     res_sq, gamma = prepare(bx - 1, prepare(0, sums))
-    start(1, (0, 1, 2, 3))
-    sums = middle(apply, (zero,) * 4)
-    arrive(1, (2, 3))
-    spread(smooth_y, smooth)
-    sums = rims(apply, sums)
-    arrive(1, (0, 1))
-    delta, cross, square, mu = ends(apply, sums, smooth, smooth_x)
-    start(2, (0, 1, 2, 3))
+    sums = ends(apply, (zero,) * 4, smooth, smooth_x)
+    start((12, 13))
+    delta, cross, square, mu = lax.fori_loop(1, bx - 1, apply, sums, unroll=STEP_UNROLL)
+    start((14, 15))
     nu = middle(apply_again, zero)
-    arrive(2, (2, 3))
+    arrive((14, 15))
     spread(scaled_y, scaled)
     nu = rims(apply_again, nu)
-    arrive(2, (0, 1))
+    arrive((12, 13))
     nu = ends(apply_again, nu, scaled, scaled_x)
 
     parts = (res_sq, gamma, delta, cross, square, mu, nu)
@@ -278,9 +320,8 @@
 
     lax.fori_loop(1, n, tell, 0)
     most = dots.at[pl.ds(0, n - 1)]
-    for phase in range(3):
-        for side in range(4):
-            pl.when(sends[side])(copies[phase][side].wait_send)
+    for side, item in copies:
+        pl.when(sends[side])(item.wait_send)
     pltpu.make_async_copy(most, most, dot_recv).wait()
 
     total = jnp.sum(jnp.sum(dots[...], axis=0), axis=1, keepdims=True)
@@ -334,7 +375,7 @@
     padded = (bx, by + 2 * PAD, nz)
     field = pltpu.VMEM(shape, f32)
     planes = pltpu.VMEM((2, by, nz), f32)
-    edges = pltpu.VMEM((2, bx, 1, nz), f32)
+    edges = pltpu.VMEM((2, bx, nz), f32)
     fields = pl.pallas_call(
         functools.partial(kernel, n),
         out_shape=tuple(
@@ -346,20 +387,25 @@
             pltpu.VMEM(shape, i32), pltpu.VMEM(padded, f32),
             pltpu.VMEM((bx + 1, by, nz), f32), pltpu.VMEM((bx, by + PAD, nz), f32),
             field, field,
-            pltpu.VMEM((2, by, nz), i32), planes, planes,
-            pltpu.VMEM((2, bx, 1, nz), i32), pltpu.VMEM((2, bx, 1, nz), i32),
-            edges, edges, edges, edges,
+            pltpu.VMEM((2, 2, by, nz), i32), planes, planes, planes,
+            pltpu.VMEM((2, 2, bx, nz), i32), pltpu.VMEM((2, 2, bx, nz), i32),
+            edges, edges, edges, edges, edges, edges,
+            pltpu.VMEM((2, 2, 1, nz), i32), pltpu.VMEM((2, 2, 1, nz), i32),
+            pltpu.VMEM((by + 2 * PAD, nz), f32), pltpu.VMEM((bx + 2 * PAD, nz), f32),
             pltpu.VMEM((n, 8, nz), f32),
             pltpu.SemaphoreType.DMA((2,)),
-            pltpu.SemaphoreType.DMA((3, 4)),
-            pltpu.SemaphoreType.DMA((3, 4)),
+            pltpu.SemaphoreType.DMA((16,)),
+            pltpu.SemaphoreType.DMA((16,)),
             pltpu.SemaphoreType.DMA,
             pltpu.SemaphoreType.DMA,
         ],
         compiler_params=pltpu.CompilerParams(
             collective_id=0, has_side_effects=True, vmem_limit_bytes=32 * 1024 * 1024
         ),
-    )(cell_kind, right_side)
+    )(
+        pltpu.with_memory_space_constraint(cell_kind, pltpu.HBM),
+        pltpu.with_memory_space_constraint(right_side, pltpu.HBM),
+    )
     x, r, norms = pl.pallas_call(
         finish,
         out_shape=(

time: 28 us -> 24.5 us (0.88)
  local copies, waits for them, and re-layouts: 2.44 us -> 0 us
  Pallas kernels: 24.8 us -> 23.7 us
    unnamed x4 -> x0, local copies, waits for them, and re-layouts: 2.44 us -> none
    pallas_call x1, Pallas kernels: 22.8 us -> 21.7 us  [body(): pl.pallas_call(functools.partial(kernel, n), out_shape=tuple((jax.ShapeDt...]
where the time goes in v3:
time: 24.5 us; the launch traced here: 24.3 us
  Pallas kernels  23.7 us (97%)
  between operations  0.64 us (3%)
    pallas_call x1, Pallas kernels, body(): pl.pallas_call(functools.partial(kernel, n), out_shape=tuple((jax.ShapeDt...  21.7 us
    pallas_call x1, Pallas kernels, body(): pl.pallas_call(finish, out_shape=(jax.ShapeDtypeStruct(right_side.shape,...  1.97 us

profile of v3, /device:TPU:0, one launch (start us, length us, event | category | flops | bytes accessed | tf_op | source)
XLA Modules:
  0.0 24.3 jit_solution(7700294712022196137)
XLA Ops:
  0.6 21.7 %shard_map.49 = (f32[32,64,128]{2,1,0:T(8,128)S(1)}, f32[32,80,128]{2,1,0:T(8,128)S(1)}, f32[32,64,128]{2,1,0:T(8,128)S(1)}, f32[32,80,128]{2,1,0:T(8,128)S(1)},...) custom-call(s32[1,32,64,128]{3,2,1,0:T(8,128)} %kind_hbm.1, f32[1,32,64,128]{3,2,1,0:T(8,128)} %right_hbm.1), custom_call_target="tpu_custom_call" | custom-call | tf_op jit(solution)/shard_map/pallas_call | solution.py:379
  22.3 2.0 %shard_map.50 = (f32[1,32,64,128]{3,2,1,0:T(8,128)}, f32[1,32,64,128]{3,2,1,0:T(8,128)}, f32[2]{0:T(128)}) custom-call(f32[32,64,128]{2,1,0:T(8,128)S(1)} %get-tuple-element.9.right, f32[32,80,128]{2,1,0:T(8,128)S(1)} %get-tuple-element.10.smooth, f32[32,64,128]{2,1,0:T(8,128)S(1)} %get-tuple-element.11.image, f32[32,80,128]{2,1,0:T(8,128)S(1)} %get-tuple-element.12.scaled, ...), custom_call_target="tpu_custom_call" | custom-call | tf_op jit(solution)/shard_map/pallas_call | solution.py:409

commit v4 on v3

--- a/solution.py
+++ b/solution.py
@@ -56,20 +56,20 @@
             sends.append(jnp.logical_and(sends[low], sends[left]))
             targets.append(targets[low] + targets[left] - me)
 
-    barrier = pltpu.get_barrier_semaphore()
-
-    def greet(k, _):
-        pl.semaphore_signal(
-            barrier, inc=1, device_id={"gx": lax.rem(me + k, n)}, device_id_type=MESH
-        )
-        return 0
-
-    lax.fori_loop(1, n, greet, 0)
-
     load_kind = pltpu.make_async_copy(kind_hbm.at[0], kind, in_sem.at[0])
     load_right = pltpu.make_async_copy(right_hbm.at[0], right, in_sem.at[1])
     load_kind.start()
     load_right.start()
+    barrier = pltpu.get_barrier_semaphore()
+
+    def greet(k, _):
+        pl.semaphore_signal(
+            barrier, inc=1, device_id={"gx": lax.rem(me + k, n)}, device_id_type=MESH
+        )
+        return 0
+
+    lax.fori_loop(1, n, greet, 0, unroll=15)
+
 
     copies = []
 
@@ -80,8 +80,8 @@
             device_id={"gx": targets[side]}, device_id_type=MESH,
         )))
 
-    copy(0, kind_hbm.at[0, pl.ds(bx - 2, 2)], kind_x.at[0])
-    copy(1, kind_hbm.at[0, pl.ds(0, 2)], kind_x.at[1])
+    copy(0, kind.at[pl.ds(bx - 2, 2)], kind_x.at[0])
+    copy(1, kind.at[pl.ds(0, 2)], kind_x.at[1])
     copy(2, send_kind_y.at[1], kind_y.at[0])
     copy(3, send_kind_y.at[0], kind_y.at[1])
     copy(0, right_hbm.at[0, bx - 1], right_x.at[0])
@@ -128,8 +128,8 @@
                 corner[side, other] = jnp.zeros((1, nz), jnp.int32)
 
     pl.semaphore_wait(barrier, n - 1)
+    load_kind.wait()
     start((0, 1, 4, 5))
-    load_kind.wait()
 
     def take_kind(i, _):
         one = pl.ds(i, 1)
@@ -355,7 +355,7 @@
             r[i] = right[i] - along * image[i] + across * second[i]
             return 0
 
-        lax.fori_loop(piece * depth, (piece + 1) * depth, combine, 0, unroll=2)
+        lax.fori_loop(piece * depth, (piece + 1) * depth, combine, 0, unroll=8)
         part = pl.ds(piece * depth, depth)
         copies.append(pltpu.make_async_copy(x.at[part], x_hbm.at[0, part], sems.at[0, piece]))
         copies.append(pltpu.make_async_copy(r.at[part], r_hbm.at[0, part], sems.at[1, piece]))

time: 24.5 us -> 24.2 us (0.988)
  Pallas kernels: 23.7 us -> 23.4 us
    pallas_call x1, Pallas kernels: 21.7 us -> 21.4 us  [body(): pl.pallas_call(functools.partial(kernel, n), out_shape=tuple((jax.ShapeDt...]
where the time goes in v4:
time: 24.2 us; the launch traced here: 24 us
  Pallas kernels  23.4 us (97%)
  between operations  0.64 us (3%)
    pallas_call x1, Pallas kernels, body(): pl.pallas_call(functools.partial(kernel, n), out_shape=tuple((jax.ShapeDt...  21.4 us
    pallas_call x1, Pallas kernels, body(): pl.pallas_call(finish, out_shape=(jax.ShapeDtypeStruct(right_side.shape,...  1.96 us

profile of v4, /device:TPU:0, one launch (start us, length us, event | category | flops | bytes accessed | tf_op | source)
XLA Modules:
  0.0 24.0 jit_solution(2229173102810276952)
XLA Ops:
  0.6 21.4 %shard_map.49 = (f32[32,64,128]{2,1,0:T(8,128)S(1)}, f32[32,80,128]{2,1,0:T(8,128)S(1)}, f32[32,64,128]{2,1,0:T(8,128)S(1)}, f32[32,80,128]{2,1,0:T(8,128)S(1)},...) custom-call(s32[1,32,64,128]{3,2,1,0:T(8,128)} %kind_hbm.1, f32[1,32,64,128]{3,2,1,0:T(8,128)} %right_hbm.1), custom_call_target="tpu_custom_call" | custom-call | tf_op jit(solution)/shard_map/pallas_call | solution.py:379
  22.1 2.0 %shard_map.50 = (f32[1,32,64,128]{3,2,1,0:T(8,128)}, f32[1,32,64,128]{3,2,1,0:T(8,128)}, f32[2]{0:T(128)}) custom-call(f32[32,64,128]{2,1,0:T(8,128)S(1)} %get-tuple-element.9.right, f32[32,80,128]{2,1,0:T(8,128)S(1)} %get-tuple-element.10.smooth, f32[32,64,128]{2,1,0:T(8,128)S(1)} %get-tuple-element.11.image, f32[32,80,128]{2,1,0:T(8,128)S(1)} %get-tuple-element.12.scaled, ...), custom_call_target="tpu_custom_call" | custom-call | tf_op jit(solution)/shard_map/pallas_call | solution.py:409

commit v5 on v4

--- a/solution.py
+++ b/solution.py
@@ -127,10 +127,7 @@
             def _():
                 corner[side, other] = jnp.zeros((1, nz), jnp.int32)
 
-    pl.semaphore_wait(barrier, n - 1)
     load_kind.wait()
-    start((0, 1, 4, 5))
-
     def take_kind(i, _):
         one = pl.ds(i, 1)
         send_kind_y[0, 0, one, :] = kind[i, 0:1, :]
@@ -143,7 +140,6 @@
     for side in (0, 1):
         for other in (0, 1):
             send_corner[side, other] = send_kind_y[other, 0, side * (bx - 1):side * (bx - 1) + 1, :]
-    start((2, 3, 8, 9, 10, 11))
     load_right.wait()
 
     def take_right(i, _):
@@ -152,7 +148,8 @@
         return 0
 
     lax.fori_loop(0, bx, take_right, 0, unroll=8)
-    start((6, 7))
+    pl.semaphore_wait(barrier, n - 1)
+    start((0, 1, 2, 3, 8, 9, 10, 11, 4, 5, 6, 7))
 
     def conduct(i, _):
         cond[i, rows] = conductivity_of(kind[i])

time: 24.2 us -> 23.9 us (0.988)
  Pallas kernels: 23.4 us -> 23.1 us
    pallas_call x1, Pallas kernels: 21.4 us -> 21.2 us  [body(): pl.pallas_call(functools.partial(kernel, n), out_shape=tuple((jax.ShapeDt...]
where the time goes in v5:
time: 23.9 us; the launch traced here: 23.8 us
  Pallas kernels  23.1 us (97%)
  between operations  0.64 us (3%)
    pallas_call x1, Pallas kernels, body(): pl.pallas_call(functools.partial(kernel, n), out_shape=tuple((jax.ShapeDt...  21.2 us
    pallas_call x1, Pallas kernels, body(): pl.pallas_call(finish, out_shape=(jax.ShapeDtypeStruct(right_side.shape,...  1.96 us

profile of v5, /device:TPU:0, one launch (start us, length us, event | category | flops | bytes accessed | tf_op | source)
XLA Modules:
  0.0 23.8 jit_solution(5590717053152974963)
XLA Ops:
  0.6 21.2 %shard_map.49 = (f32[32,64,128]{2,1,0:T(8,128)S(1)}, f32[32,80,128]{2,1,0:T(8,128)S(1)}, f32[32,64,128]{2,1,0:T(8,128)S(1)}, f32[32,80,128]{2,1,0:T(8,128)S(1)},...) custom-call(s32[1,32,64,128]{3,2,1,0:T(8,128)} %kind_hbm.1, f32[1,32,64,128]{3,2,1,0:T(8,128)} %right_hbm.1), custom_call_target="tpu_custom_call" | custom-call | tf_op jit(solution)/shard_map/pallas_call | solution.py:376
  21.8 2.0 %shard_map.50 = (f32[1,32,64,128]{3,2,1,0:T(8,128)}, f32[1,32,64,128]{3,2,1,0:T(8,128)}, f32[2]{0:T(128)}) custom-call(f32[32,64,128]{2,1,0:T(8,128)S(1)} %get-tuple-element.9.right, f32[32,80,128]{2,1,0:T(8,128)S(1)} %get-tuple-element.10.smooth, f32[32,64,128]{2,1,0:T(8,128)S(1)} %get-tuple-element.11.image, f32[32,80,128]{2,1,0:T(8,128)S(1)} %get-tuple-element.12.scaled, ...), custom_call_target="tpu_custom_call" | custom-call | tf_op jit(solution)/shard_map/pallas_call | solution.py:406
